TPU v7x, 32 devices: a whole 2x2x4 slice. The times are simulated.
32 devices in a mesh: fac: 8 (over y, x, core), loc: 4 (over z).
Axes of the slice: x: 2, y: 2, z: 4, core: 2. Of those that a mesh axis runs over, the one named last changes fastest.
Arguments:
- quad_cost: float32 [128, 128, 128, 128], P('fac', 'loc'), may hold values from -30 to 30
- leader: float32 [128, 128], P('fac', 'loc'), may hold values from -4 to 4
Outputs:
- new_cost: float32 [128, 128, 128, 128], P('fac', 'loc')
- new_leader: float32 [128, 128], P('fac', 'loc')
All inputs are finite; a program needn't handle non-finite values.
Results may differ from a plain program's by a relative error of at most 0.0001.
Values sent between devices are 32-bit elements; how exact they have to be, the bound alone decides.
A program may use at most 448 MiB of HBM per device.

v0:
```python
import jax
import jax.numpy as jnp
from jax import lax
from jax.sharding import PartitionSpec as P

N = 128
SWEEPS = 3


temper = 0.15
leader_temper = 0.1


def combined_all(x, axis, combine):
    everything = jax.tree.map(lambda part: lax.all_gather(part, axis), x)
    initial = jax.tree.map(lambda part: part[0], everything)

    def hop(k, so_far):
        return combine(so_far, jax.tree.map(lambda part: part[k], everything))

    return lax.fori_loop(1, lax.axis_size(axis), hop, initial)


def soft_min(values, axis, scale):
    scaled = -values / scale
    highest = jnp.max(scaled, axis=axis, keepdims=True)
    totals = jnp.sum(jnp.exp(scaled - highest), axis=axis, keepdims=True)
    return jnp.squeeze(-scale * (highest + jnp.log(totals)), axis)


def partial_totals(values, axis):
    scaled = -values / leader_temper
    highest = jnp.max(scaled, axis=axis)
    totals = jnp.sum(jnp.exp(scaled - jnp.expand_dims(highest, axis)), axis=axis)
    return (highest, totals)


def join_totals(first, second):
    highest = jnp.maximum(first[0], second[0])
    totals = first[1] * jnp.exp(first[0] - highest) + second[1] * jnp.exp(second[0] - highest)
    return (highest, totals)


def sweep_block(block):
    col_dual = jnp.zeros(block.shape[:-2] + (block.shape[-1],), jnp.float32)
    row_dual = jnp.zeros(block.shape[:-1], jnp.float32)
    for sweep in range(SWEEPS):
        row_dual = soft_min(block - col_dual[..., None, :], -1, temper)
        col_dual = soft_min(block - row_dual[..., :, None], -2, temper)
    reduced = block - row_dual[..., :, None] - col_dual[..., None, :]
    worth = (jnp.sum(row_dual, -1) + jnp.sum(col_dual, -1)) / N
    return (reduced, worth)


def on_device(quad_cost, leader):
    fac_rows = quad_cost.shape[0]
    loc_rows = quad_cost.shape[1]
    fac_count = lax.axis_size("fac")
    loc_count = lax.axis_size("loc")
    reduced, worth = sweep_block(quad_cost)
    outgoing = reduced.reshape(fac_rows, loc_rows, fac_count, fac_rows, loc_count, loc_rows)
    outgoing = outgoing.transpose(2, 4, 3, 5, 0, 1).reshape(
        fac_count, loc_count, fac_rows, loc_rows, fac_rows * loc_rows
    )
    flat_out = outgoing.reshape(fac_count * loc_count, fac_rows, loc_rows, fac_rows * loc_rows)
    incoming = lax.all_to_all(flat_out, ("fac", "loc"), split_axis=0, concat_axis=0, tiled=True)
    partner = incoming.reshape(fac_count, loc_count, fac_rows, loc_rows, fac_rows, loc_rows)
    partner = partner.transpose(2, 3, 0, 4, 1, 5).reshape(fac_rows, loc_rows, N, N)
    quad_cost = 0.5 * (reduced + partner)
    leader = leader + worth
    highest, totals = combined_all(partial_totals(leader, 1), "loc", join_totals)
    leader = leader - (-leader_temper * (highest + jnp.log(totals)))[:, None]
    highest, totals = combined_all(partial_totals(leader, 0), "fac", join_totals)
    leader = leader - (-leader_temper * (highest + jnp.log(totals)))[None, :]
    return (quad_cost, leader)


def solution(mesh):
    return jax.shard_map(
        on_device,
        mesh=mesh,
        in_specs=(P("fac", "loc", None, None), P("fac", "loc")),
        out_specs=(P("fac", "loc", None, None), P("fac", "loc")),
        check_vma=False,
    )
```

profile of v0, /device:TPU:29, one launch (start us, length us, event | category | flops | bytes accessed | tf_op | source)
XLA Modules:
  0.0 1675.7 jit_solution(10003257898323965763)
XLA Ops:
  0.6 15.3 fusion.4
  15.9 20.6 %exponential_reduce_fusion.5 = f32[16,32,128]{2,1,0:T(8,128)S(1)} fusion(f32[16,32,128,128]{3,2,1,0:T(8,128)} %param.6, f32[16,32,128]{2,1,0:T(8,128)S(1)} %fusion.4), kind=kLoop, calls=%fused_computation.23 | loop fusion | flops 33488896 | bytes 34078720 | tf_op jit(solution)/shard_map/reduce_sum | solution.py:27
  36.5 0.1 add_multiply_fusion.6
  36.6 12.1 fusion.5
  48.7 13.2 exponential_reduce_fusion.4
  61.9 0.1 add_multiply_fusion.5
  62.0 15.3 fusion.6
  77.2 21.2 %exponential_reduce_fusion.3 = f32[16,32,128]{2,1,0:T(8,128)S(1)} fusion(f32[16,32,128,128]{3,2,1,0:T(8,128)} %param.6, f32[16,32,128]{2,1,0:T(8,128)S(1)} %fusion.6, f32[16,32,128]{2,1,0:T(8,128)S(1)} %add_multiply_fusion.5), kind=kLoop, calls=%fused_computation.19 | loop fusion | flops 41877504 | bytes 34340864 | tf_op jit(solution)/shard_map/reduce_sum | solution.py:27
  98.4 0.1 add_multiply_fusion.4
  98.5 12.1 fusion.7
  110.6 13.2 exponential_reduce_fusion.2
  123.8 0.1 add_multiply_fusion.3
  123.9 15.3 fusion.8
  139.2 21.2 %exponential_reduce_fusion.1 = f32[16,32,128]{2,1,0:T(8,128)S(1)} fusion(f32[16,32,128,128]{3,2,1,0:T(8,128)} %param.6, f32[16,32,128]{2,1,0:T(8,128)S(1)} %fusion.8, f32[16,32,128]{2,1,0:T(8,128)S(1)} %add_multiply_fusion.3), kind=kLoop, calls=%fused_computation.15 | loop fusion | flops 41877504 | bytes 34340864 | tf_op jit(solution)/shard_map/reduce_sum | solution.py:27
  160.4 0.8 fusion.13
  161.1 12.1 fusion.9
  173.3 13.2 exponential_reduce_fusion
  186.5 0.7 fusion.12
  187.2 0.7 copy-done.2
  187.9 23.1 %subtract_subtract_fusion = f32[16,32,128,128]{3,2,1,0:T(8,128)} fusion(f32[16,32,128,128]{3,2,1,0:T(8,128)} %param.6, f32[16,32,128]{2,1,0:T(8,128)S(1)} %get-tuple-element.303, f32[16,32,128]{2,1,0:T(8,128)S(1)} %get-tuple-element.305), kind=kLoop, calls=%fused_computation.25 | loop fusion | flops 16777216 | bytes 67633152 | tf_op jit(solution)/shard_map/sub | solution.py:50
  211.0 90.6 %reshape.83 = f32[16,32,8,16,4,32]{5,4,3,2,1,0:T(4,128)} reshape(f32[16,32,128,128]{3,2,1,0:T(8,128)} %subtract_subtract_fusion) | data formatting | bytes 67108864 | tf_op jit(solution)/shard_map/reshape | solution.py:61
  301.6 155.3 %copy.5 = f32[16,32,8,16,4,32]{1,0,5,3,4,2:T(8,128)} copy(f32[16,32,8,16,4,32]{5,4,3,2,1,0:T(4,128)} %reshape.83) | data formatting | bytes 67108864 | tf_op jit(solution)/shard_map/reshape | solution.py:61
  456.9 95.7 %reshape_reshape.3 = f32[32,16,32,512]{3,2,1,0:T(8,128)} reshape(f32[8,4,16,32,16,32]{5,4,3,2,1,0:T(8,128)} %bitcast.4) | data formatting | bytes 67108864 | tf_op jit(solution)/shard_map/reshape;reshape | solution.py:65
  552.6 0.0 copy-start.6
  552.6 6.2 all-to-all-start
  558.9 0.6 dynamic-slice.2
  559.5 0.6 dynamic-slice
  560.8 0.1 fusion.10
  560.9 0.2 dynamic-update-slice
  561.2 0.2 exponential_reduce_fusion.7
  561.4 0.2 dynamic-update-slice.1
  561.6 742.5 %all-reduce.5 = (f32[64]{0:T(128)S(1)}, f32[64]{0:T(128)S(1)}) all-reduce(f32[64]{0:T(128)S(1)} %dynamic-update-slice, f32[64]{0:T(128)S(1)} %dynamic-update-slice.1), channel_id=2, replica_groups=mesh['fac'=8,'loc'=4] {'loc'}, use_global_device_ids=true, to_apply=%add | all-reduce | flops 128 | bytes 1024
  1304.1 0.1 reshape.86
  1304.2 0.1 reshape.87
  1305.0 0.1 while.34
  1305.1 0.1 fusion.11
  1305.2 0.2 dynamic-update-slice.2
  1305.5 0.1 exponential_reduce_fusion.6
  1305.6 0.2 dynamic-update-slice.3
  1305.8 13.2 all-reduce.4
  1319.0 0.1 reshape.89
  1319.1 0.1 reshape.88
  1319.2 0.3 while.35
  1319.5 0.7 subtract_subtract_fusion.1
  1320.2 79.7 %reshape.84 = f32[8,4,16,32,16,32]{5,4,3,2,1,0:T(8,128)} reshape(f32[32,16,32,512]{3,2,1,0:T(8,128)} %all-to-all-done) | data formatting | bytes 67108864 | tf_op jit(solution)/shard_map/reshape | solution.py:67
  1399.8 143.3 %copy.6 = f32[16,32,8,16,4,32]{5,4,3,2,1,0:T(4,128)} copy(f32[16,32,8,16,4,32]{5,3,1,0,4,2:T(8,128)} %bitcast.5) | data formatting | bytes 67108864 | tf_op jit(solution)/shard_map/transpose | solution.py:68
  1543.1 99.0 %reshape.85 = f32[16,32,128,128]{3,2,1,0:T(8,128)} reshape(f32[16,32,8,16,4,32]{5,4,3,2,1,0:T(4,128)} %copy.6) | data formatting | bytes 67108864 | tf_op jit(solution)/shard_map/reshape | solution.py:68
  1642.1 33.6 %add_multiply_fusion = f32[16,32,128,128]{3,2,1,0:T(8,128)} fusion(f32[16,32,128,128]{3,2,1,0:T(8,128)} %reshape.85, f32[16,32,128]{2,1,0:T(8,128)S(1)} %copy-done.3, f32[16,32,128,128]{3,2,1,0:T(8,128)} %param.6, f32[16,32,128]{2,1,0:T(8,128)S(1)} %copy-done.1), kind=kLoop, calls=%fused_computation.12 | loop fusion | flops 33554432 | bytes 101187584 | tf_op jit(solution)/shard_map/mul | solution.py:69
  (35 shorter events, 0.3 us)
Async XLA Ops:
  161.1 26.1 %copy-start = (f32[16,32,128]{2,1,0:T(8,128)}, f32[16,32,128]{2,1,0:T(8,128)S(1)}, u32[]{:S(2)}) copy-start(f32[16,32,128]{2,1,0:T(8,128)S(1)} %get-tuple-element.305) | copy-start | bytes 786436
  187.2 0.7 copy-start.2
  552.6 6.3 copy-start.8
  552.6 6.9 copy-start.7
  552.6 8.2 copy-start.4
  552.6 8.2 copy-start.5
  552.6 8.2 copy-start.6
  552.6 767.5 %all-to-all-start = ((f32[32,16,32,512]{3,2,1,0:T(8,128)}), f32[32,16,32,512]{3,2,1,0:T(8,128)}, u32[]{:S(2)}, u32[]{:S(2)}) async-start(f32[32,16,32,512]{3,2,1,0:T(8,128)} %reshape_reshape.3), calls=%async_computation | async-start | bytes 67108864 | tf_op jit(solution)/shard_map/all_to_all | solution.py:66
  1543.1 99.0 %copy-start.1 = (f32[16,32,128]{2,1,0:T(8,128)S(1)}, f32[16,32,128]{2,1,0:T(8,128)}, u32[]{:S(2)}) copy-start(f32[16,32,128]{2,1,0:T(8,128)} %copy-done) | copy-start | bytes 786436
  1543.1 99.0 %copy-start.3 = (f32[16,32,128]{2,1,0:T(8,128)S(1)}, f32[16,32,128]{2,1,0:T(8,128)}, u32[]{:S(2)}) copy-start(f32[16,32,128]{2,1,0:T(8,128)} %copy-done.2) | copy-start | bytes 786436
where the time goes:
time: 1690 us; the launch traced here: 1680 us
  blocking collectives  756 us (45%)
  local copies, waits for them, and re-layouts  667 us (39%)
  other arithmetic  245 us (14%)
    unnamed x2, blocking collectives  756 us
    reshape x2, local copies, waits for them, and re-layouts, on_device(): reduced.reshape(fac_rows, loc_rows, fac_count, fac_rows, loc_count, loc_r...  246 us
    transpose x1, local copies, waits for them, and re-layouts, on_device(): partner.transpose(2, 3, 0, 4, 1, 5).reshape(fac_rows, loc_rows, N, N)  143 us
    reduce_sum x6, other arithmetic, soft_min(): totals = jnp.sum(jnp.exp(scaled - highest), axis=axis, keepdims=True)  103 us
    reshape x1, local copies, waits for them, and re-layouts, on_device(): partner.transpose(2, 3, 0, 4, 1, 5).reshape(fac_rows, loc_rows, N, N)  99 us
    another operation x1, local copies, waits for them, and re-layouts, on_device(): outgoing.reshape(fac_count * loc_count, fac_rows, loc_rows, fac_rows * lo...  95.7 us
    reduce_max x6, other arithmetic, soft_min(): highest = jnp.max(scaled, axis=axis, keepdims=True)  82.2 us
    reshape x1, local copies, waits for them, and re-layouts, on_device(): incoming.reshape(fac_count, loc_count, fac_rows, loc_rows, fac_rows, loc_...  79.7 us
  transfers between devices with their start and end apart: 1, of which 0 were waited for; matrix products, arithmetic and copies ran while one was open for 0% of the time, Pallas kernels for 0%

commit v1 on v0

v1 whole, which is shorter than its diff:
```python
import functools
import math

import jax
import jax.numpy as jnp
from jax import lax
from jax.experimental import pallas as pl
from jax.experimental.pallas import tpu as pltpu
from jax.sharding import PartitionSpec as P

SWEEPS = 3

temper = 0.15
leader_temper = 0.1

SCALE = 1.0 / (temper * math.log(2.0))
LOG2E = 1.0 / math.log(2.0)
GROUP = 8


def combined_all(x, axis, combine):
    everything = jax.tree.map(lambda part: lax.all_gather(part, axis), x)
    initial = jax.tree.map(lambda part: part[0], everything)

    def hop(k, so_far):
        return combine(so_far, jax.tree.map(lambda part: part[k], everything))

    return lax.fori_loop(1, lax.axis_size(axis), hop, initial)


def partial_totals(values, axis):
    scaled = -values / leader_temper
    highest = jnp.max(scaled, axis=axis)
    totals = jnp.sum(jnp.exp(scaled - jnp.expand_dims(highest, axis)), axis=axis)
    return (highest, totals)


def join_totals(first, second):
    highest = jnp.maximum(first[0], second[0])
    totals = first[1] * jnp.exp(first[0] - highest) + second[1] * jnp.exp(second[0] - highest)
    return (highest, totals)


def swap_lane_groups(rows, width):
    rows = list(rows)
    count = len(rows)
    lane_group = lax.broadcasted_iota(jnp.int32, rows[0].shape, 1) // width
    lanes = rows[0].shape[1]
    dist = count // 2
    while dist:
        low = (lane_group // dist) % 2 == 0
        for r in range(count):
            if (r // dist) % 2 == 0:
                a, b = rows[r], rows[r + dist]
                rows[r] = jnp.where(low, a, pltpu.roll(b, dist * width, 1))
                rows[r + dist] = jnp.where(low, pltpu.roll(a, lanes - dist * width, 1), b)
        dist //= 2
    return rows


def sweep_kernel(loc_count, with_prior, *refs):
    if with_prior:
        c_ref, _, r_ref, send_ref, w_ref, p_s, z_s = refs
    else:
        c_ref, r_ref, send_ref, w_ref, p_s, z_s = refs
    n = c_ref.shape[1]
    width = n // loc_count
    per_fac = send_ref.shape[3]
    batch = 64
    shape = (GROUP, n)

    zero = jnp.zeros(shape, jnp.float32)

    def first_rows(step, top_and_sum):
        top, u_sum = top_and_sum
        k0 = step * batch
        ys = [c_ref[pl.ds(k0 + t, GROUP, stride=n), :] * (-SCALE) for t in range(batch)]
        highs = [jnp.max(y, axis=1, keepdims=True) for y in ys]
        sums = [jnp.sum(jnp.exp2(y - h), axis=1, keepdims=True) for y, h in zip(ys, highs)]
        us = [-(h + jnp.log(s) * LOG2E) for h, s in zip(highs, sums)]
        for t in range(batch):
            z = ys[t] + us[t]
            z_s[k0 + t] = z
            top = jnp.maximum(top, z)
            u_sum = u_sum + us[t]
        return top, u_sum

    top, u_sum = lax.fori_loop(
        0, n // batch, first_rows,
        (jnp.full(shape, -jnp.inf, jnp.float32), jnp.zeros((GROUP, 1), jnp.float32)),
    )

    def first_columns(step, totals):
        k0 = step * batch
        totals = list(totals)
        for t in range(batch):
            e = jnp.exp2(z_s[k0 + t] - top)
            p_s[k0 + t] = e
            totals[t % 4] = totals[t % 4] + e
        return tuple(totals)

    totals = lax.fori_loop(0, n // batch, first_columns, (zero,) * 4)
    total = (totals[0] + totals[1]) + (totals[2] + totals[3])

    weight = 1.0 / total
    for sweep in range(1, SWEEPS):
        last = sweep == SWEEPS - 1

        def later(step, totals, weight=weight, last=last):
            k0 = step * batch
            totals = list(totals)
            ps = [p_s[k0 + t] for t in range(batch)]
            sums = [jnp.sum(p * weight, axis=1, keepdims=True) for p in ps]
            for t in range(batch):
                totals[t % 4] = totals[t % 4] + ps[t] * (1.0 / sums[t])
            if last:
                for t in range(batch):
                    drop = jnp.log(sums[t]) * LOG2E
                    z_s[k0 + t] = z_s[k0 + t] - drop
                    totals[4] = totals[4] - drop
            return tuple(totals)

        start = (zero,) * 4 + ((u_sum,) if last else ())
        totals = lax.fori_loop(0, n // batch, later, start)
        total = (totals[0] + totals[1]) + (totals[2] + totals[3])
        weight = 1.0 / total
        if last:
            u_sum = totals[4]
    col = -(top + jnp.log(total) * LOG2E)

    worth = (u_sum + jnp.sum(col, axis=1, keepdims=True)) * (1.0 / (SCALE * n))
    w_ref[0] = jnp.broadcast_to(worth, shape)

    def finish(q, carry):
        k0 = q * loc_count
        outs = []
        for t in range(loc_count):
            r = (z_s[k0 + t] + col) * (-1.0 / SCALE)
            r_ref[pl.ds(k0 + t, GROUP, stride=n), :] = r
            outs.append(r)
        for b, packed in enumerate(swap_lane_groups(outs, width)):
            send_ref[q // per_fac, b, 0, q % per_fac] = packed
        return carry

    lax.fori_loop(0, n // loc_count, finish, 0, unroll=2)


def sweep_chunk(cost, prior, start, size, fac_rows, loc_rows, fac_count, loc_count):
    n = cost.shape[1]
    groups = loc_rows // GROUP
    per_fac = fac_rows // loc_count
    rows = GROUP * n
    elements = size * loc_rows * n * n
    in_specs = [pl.BlockSpec((rows, n), lambda i, g: ((i + start) * groups + g, 0))]
    operands = [cost]
    aliases = {}
    if prior is not None:
        in_specs.append(pl.BlockSpec(memory_space=pl.ANY))
        operands.append(prior)
        aliases = {1: 0}
    return pl.pallas_call(
        functools.partial(sweep_kernel, loc_count, prior is not None),
        grid=(size, groups),
        in_specs=in_specs,
        out_specs=[
            pl.BlockSpec((rows, n), lambda i, g: ((i + start) * groups + g, 0)),
            pl.BlockSpec(
                (fac_count, loc_count, 1, per_fac, GROUP, n), lambda i, g: (0, 0, i, 0, g, 0)
            ),
            pl.BlockSpec((1, GROUP, n), lambda i, g: (i, g, 0)),
        ],
        out_shape=[
            jax.ShapeDtypeStruct(cost.shape, jnp.float32),
            jax.ShapeDtypeStruct(
                (fac_count, loc_count, size, per_fac, loc_rows, n), jnp.float32
            ),
            jax.ShapeDtypeStruct((size, loc_rows, n), jnp.float32),
        ],
        scratch_shapes=[
            pltpu.VMEM((n, GROUP, n), jnp.float32),
            pltpu.VMEM((n, GROUP, n), jnp.float32),
        ],
        input_output_aliases=aliases,
        compiler_params=pltpu.CompilerParams(vmem_limit_bytes=24 * 1024 * 1024),
        cost_estimate=pl.CostEstimate(
            flops=elements * 40, bytes_accessed=elements * 12, transcendentals=elements * 6
        ),
        name="sweeps",
    )(*operands)


def join_kernel(sizes, pad, *refs):
    parts = refs[: len(sizes)]
    r_ref, o_ref, s_ref = refs[len(sizes):]
    fac_step, loc_count = parts[0].shape[0], parts[0].shape[1]
    width, rows = r_ref.shape[1], r_ref.shape[2]
    at = 0
    for f in range(fac_step):
        for part, size in zip(parts, sizes):
            for i in range(size):
                tile = jnp.concatenate([part[f, b, i, 0] for b in range(loc_count)], axis=0)
                s_ref[pl.ds(at * pad, tile.shape[1]), :] = tile.T
                at += 1

    for t in range(loc_count):

        def step(l, carry, t=t):
            partner = s_ref[pl.ds(t * width + l, rows, stride=pad), :]
            o_ref[t, l] = 0.5 * (r_ref[t, l] + partner)
            return carry

        lax.fori_loop(0, width, step, 0, unroll=8)


def join_chunks(reduced, parts, sizes, fac_rows, loc_rows, fac_count, loc_count):
    n = reduced.shape[2]
    fac_step = max(1, 8 // fac_rows)
    rows = fac_step * fac_rows
    per_fac = fac_rows // loc_count
    pad = n + 8
    own = pl.BlockSpec((loc_count, loc_rows, rows, n), lambda q, f: (q, 0, f, 0))
    return pl.pallas_call(
        functools.partial(join_kernel, sizes, pad),
        grid=(per_fac, fac_count // fac_step),
        in_specs=[
            pl.BlockSpec(
                (fac_step, loc_count, size, 1, loc_rows, n), lambda q, f: (f, 0, 0, q, 0, 0)
            )
            for size in sizes
        ]
        + [own],
        out_specs=own,
        out_shape=jax.ShapeDtypeStruct(reduced.shape, jnp.float32),
        scratch_shapes=[pltpu.VMEM((rows * pad, n), jnp.float32)],
        compiler_params=pltpu.CompilerParams(vmem_limit_bytes=24 * 1024 * 1024),
        cost_estimate=pl.CostEstimate(
            flops=reduced.size * 4, bytes_accessed=reduced.size * 12, transcendentals=0
        ),
        name="join",
    )(*parts, reduced)


def chunk_sizes(rows):
    sizes, left, size = [], rows, 1
    while left > 2 * size + 1:
        sizes.append(size)
        left -= size
        size *= 2
    return tuple(sizes) + (left,)


def on_device(quad_cost, leader):
    fac_rows, loc_rows, n, _ = quad_cost.shape
    fac_count = lax.axis_size("fac")
    loc_count = lax.axis_size("loc")
    flat = quad_cost.reshape(fac_rows * loc_rows * n, n)
    sizes = chunk_sizes(fac_rows)
    reduced, start = None, 0
    parts, worths = [], []
    for size in sizes:
        reduced, outgoing, worth = sweep_chunk(
            flat, reduced, start, size, fac_rows, loc_rows, fac_count, loc_count
        )
        shape = outgoing.shape
        outgoing = outgoing.reshape((fac_count * loc_count,) + shape[2:])
        incoming = lax.all_to_all(outgoing, ("fac", "loc"), split_axis=0, concat_axis=0, tiled=True)
        parts.append(incoming.reshape(shape))
        worths.append(worth[:, :, 0])
        start += size
    new_cost = join_chunks(
        reduced.reshape(quad_cost.shape), parts, sizes, fac_rows, loc_rows, fac_count, loc_count
    )
    leader = leader + jnp.concatenate(worths, axis=0)
    highest, totals = combined_all(partial_totals(leader, 1), "loc", join_totals)
    leader = leader - (-leader_temper * (highest + jnp.log(totals)))[:, None]
    highest, totals = combined_all(partial_totals(leader, 0), "fac", join_totals)
    leader = leader - (-leader_temper * (highest + jnp.log(totals)))[None, :]
    return (new_cost, leader)


def solution(mesh):
    return jax.shard_map(
        on_device,
        mesh=mesh,
        in_specs=(P("fac", "loc", None, None), P("fac", "loc")),
        out_specs=(P("fac", "loc", None, None), P("fac", "loc")),
        check_vma=False,
    )
```

time: 1690 us -> 850 us (0.50)
  local copies, waits for them, and re-layouts: 667 us -> 16.3 us
  blocking collectives: 756 us -> 429 us
  Pallas kernels: 0 us -> 313 us
  other arithmetic: 245 us -> 1.44 us
  waiting for transfers between devices: 0.01 us -> 53.2 us
  starting transfers between devices: 6.22 us -> 34.3 us
    reshape x4 -> x0, local copies, waits for them, and re-layouts: 425 us -> none  [the longest x2 246 us: on_device(): reduced.reshape(fac_rows, loc_rows, fac_count, fac_rows, loc_count, loc_r...]
    unnamed x2, blocking collectives: 756 us -> 429 us
    pallas_call x0 -> x5, Pallas kernels: none -> 313 us  [the longest x4 264 us: sweep_chunk(): pl.pallas_call(functools.partial(sweep_kernel, loc_count, prior is not No...]
    transpose x1 -> x0, local copies, waits for them, and re-layouts: 143 us -> none  [on_device(): partner.transpose(2, 3, 0, 4, 1, 5).reshape(fac_rows, loc_rows, N, N)]
    reduce_sum x8 -> x0, other arithmetic: 104 us -> none  [the longest x6 103 us: soft_min(): totals = jnp.sum(jnp.exp(scaled - highest), axis=axis, keepdims=True)]
    another operation x1 -> x0, local copies, waits for them, and re-layouts: 95.7 us -> none  [on_device(): outgoing.reshape(fac_count * loc_count, fac_rows, loc_rows, fac_rows * lo...]
    reduce_max x6 -> x0, other arithmetic: 82.2 us -> none  [soft_min(): highest = jnp.max(scaled, axis=axis, keepdims=True)]
    all_to_all x1 -> x4, waiting for transfers between devices: 0.01 us -> 53.2 us  [on_device(): lax.all_to_all(outgoing, ('fac', 'loc'), split_axis=0, concat_axis=0, til...]
  transfers between devices with their start and end apart: 1 -> 4, of which waited for: 0 -> 3; matrix products, arithmetic and copies ran while one was open for 0% -> 1% of each run, Pallas kernels for 0% -> 29%
where the time goes in v1:
time: 850 us; the launch traced here: 849 us
  blocking collectives  429 us (50%)
  Pallas kernels  313 us (37%)
  waiting for transfers between devices  53.2 us (6%)
  starting transfers between devices  34.3 us (4%)
  local copies, waits for them, and re-layouts  16.3 us (2%)
    unnamed x2, blocking collectives  429 us
    pallas_call x4, Pallas kernels, sweep_chunk(): pl.pallas_call(functools.partial(sweep_kernel, loc_count, prior is not No...  264 us
    all_to_all x4, waiting for transfers between devices, on_device(): lax.all_to_all(outgoing, ('fac', 'loc'), split_axis=0, concat_axis=0, til...  53.2 us
    pallas_call x1, Pallas kernels, join_chunks(): pl.pallas_call(functools.partial(join_kernel, sizes, pad), grid=(per_fac,...  48.8 us
    all_to_all x4, starting transfers between devices, on_device(): lax.all_to_all(outgoing, ('fac', 'loc'), split_axis=0, concat_axis=0, til...  34.3 us
  transfers between devices with their start and end apart: 4, of which 3 were waited for; matrix products, arithmetic and copies ran while one was open for 1% of the time, Pallas kernels for 29%

profile of v1, /device:TPU:29, one launch (start us, length us, event | category | flops | bytes accessed | tf_op | source)
XLA Modules:
  0.0 849.1 jit_solution(435096462463008260)
XLA Ops:
  0.6 17.8 %sweeps.4 = (f32[65536,128]{1,0:T(8,128)}, f32[8,4,1,4,32,128]{5,4,3,2,1,0:T(8,128)S(1)}, f32[1,32,128]{2,1,0:T(8,128)S(1)}) custom-call(f32[65536,128]{1,0:T(8,128)} %bitcast.51), custom_call_target="tpu_custom_call" | custom-call | flops 20971520 | bytes 6291456 | tf_op jit(solution)/shard_map/sweeps/pallas_call | solution.py:161
  18.4 0.0 copy-start.3
  18.4 1.3 copy-done.3
  19.7 6.2 all-to-all-start
  25.9 33.9 %sweeps.5 = (f32[65536,128]{1,0:T(8,128)}, f32[8,4,2,4,32,128]{5,4,3,2,1,0:T(8,128)S(1)}, f32[2,32,128]{2,1,0:T(8,128)S(1)}) custom-call(f32[65536,128]{1,0:T(8,128)} %bitcast.52, f32[65536,128]{1,0:T(8,128)} %get-tuple-element.281.refs_1_), custom_call_target="tpu_custom_call", output_to_operand_aliasing={{0}: (1, {})} | custom-call | flops 41943040 | bytes 12582912 | tf_op jit(solution)/shard_map/sweeps/pallas_call | solution.py:161
  59.8 0.0 copy-start.2
  59.8 2.0 copy-done.2
  61.8 9.6 %all-to-all-done = f32[32,1,4,32,128]{4,3,2,1,0:T(8,128)S(1)} async-done(((f32[32,1,4,32,128]{4,3,2,1,0:T(8,128)}), f32[32,1,4,32,128]{4,3,2,1,0:T(8,128)S(1)}, u32[]{:S(2)}, u32[]{:S(2)}) %all-to-all-start) | async-done | bytes 2097184 | tf_op jit(solution)/shard_map/all_to_all | solution.py:266
  71.4 6.2 all-to-all-start.1
  77.6 66.0 %sweeps.6 = (f32[65536,128]{1,0:T(8,128)}, f32[8,4,4,4,32,128]{5,4,3,2,1,0:T(8,128)S(1)}, f32[4,32,128]{2,1,0:T(8,128)S(1)}) custom-call(f32[65536,128]{1,0:T(8,128)} %bitcast.53, f32[65536,128]{1,0:T(8,128)} %get-tuple-element.283.refs_1_), custom_call_target="tpu_custom_call", output_to_operand_aliasing={{0}: (1, {})} | custom-call | flops 83886080 | bytes 25165824 | tf_op jit(solution)/shard_map/sweeps/pallas_call | solution.py:161
  143.6 3.2 copy-done.1
  146.8 20.1 %all-to-all-done.1 = f32[32,2,4,32,128]{4,3,2,1,0:T(8,128)} async-done(((f32[32,2,4,32,128]{4,3,2,1,0:T(8,128)}), f32[32,2,4,32,128]{4,3,2,1,0:T(8,128)}, u32[]{:S(2)}, u32[]{:S(2)}) %all-to-all-start.1) | async-done | bytes 4194336 | tf_op jit(solution)/shard_map/all_to_all | solution.py:266
  166.9 8.7 %all-to-all-start.2 = ((f32[32,4,4,32,128]{4,3,2,1,0:T(8,128)}), f32[32,4,4,32,128]{4,3,2,1,0:T(8,128)}, u32[]{:S(2)}, u32[]{:S(2)}) async-start(f32[32,4,4,32,128]{4,3,2,1,0:T(8,128)} %bitcast.47), calls=%async_computation.2 | async-start | bytes 16777216 | tf_op jit(solution)/shard_map/all_to_all | solution.py:266
  175.6 146.3 %sweeps.7 = (f32[65536,128]{1,0:T(8,128)}, f32[8,4,9,4,32,128]{5,4,3,2,1,0:T(8,128)S(1)}, f32[9,32,128]{2,1,0:T(8,128)S(1)}) custom-call(f32[65536,128]{1,0:T(8,128)} %bitcast.54, f32[65536,128]{1,0:T(8,128)} %get-tuple-element.285.refs_1_), custom_call_target="tpu_custom_call", output_to_operand_aliasing={{0}: (1, {})} | custom-call | flops 188743680 | bytes 56623104 | tf_op jit(solution)/shard_map/sweeps/pallas_call | solution.py:161
  321.9 0.0 copy-start
  321.9 6.8 copy-done
  328.7 23.6 %all-to-all-done.2 = f32[32,4,4,32,128]{4,3,2,1,0:T(8,128)} async-done(((f32[32,4,4,32,128]{4,3,2,1,0:T(8,128)}), f32[32,4,4,32,128]{4,3,2,1,0:T(8,128)}, u32[]{:S(2)}, u32[]{:S(2)}) %all-to-all-start.2) | async-done | bytes 8388640 | tf_op jit(solution)/shard_map/all_to_all | solution.py:266
  352.3 0.0 copy-start.6
  352.3 0.0 copy-start.5
  352.3 13.3 %all-to-all-start.3 = ((f32[32,9,4,32,128]{4,3,2,1,0:T(8,128)}), f32[32,9,4,32,128]{4,3,2,1,0:T(8,128)}, u32[]{:S(2)}, u32[]{:S(2)}) async-start(f32[32,9,4,32,128]{4,3,2,1,0:T(8,128)} %bitcast.45), calls=%async_computation.3 | async-start | bytes 37748736 | tf_op jit(solution)/shard_map/all_to_all | solution.py:266
  365.6 0.0 copy-done.6
  365.6 0.7 dynamic-slice.2
  366.2 0.0 copy-done.5
  366.2 0.6 dynamic-slice
  367.5 0.1 slice_reduce_fusion.3
  367.6 0.1 slice_reduce_fusion.2
  367.7 0.1 slice_reduce_fusion.1
  367.8 0.1 slice_reduce_fusion
  367.9 0.0 copy-done.4
  367.9 0.1 fusion.4
  368.0 0.2 dynamic-update-slice
  368.3 0.2 exponential_reduce_fusion.1
  368.5 0.2 dynamic-update-slice.1
  368.7 415.6 %all-reduce.5 = (f32[64]{0:T(128)S(1)}, f32[64]{0:T(128)S(1)}) all-reduce(f32[64]{0:T(128)S(1)} %dynamic-update-slice, f32[64]{0:T(128)S(1)} %dynamic-update-slice.1), channel_id=2, replica_groups=mesh['fac'=8,'loc'=4] {'loc'}, use_global_device_ids=true, to_apply=%add | all-reduce | flops 128 | bytes 1024
  784.3 0.1 reshape.48
  784.4 0.1 reshape.49
  785.2 0.1 while.34
  785.3 0.1 fusion.5
  785.4 0.2 dynamic-update-slice.2
  785.6 0.1 exponential_reduce_fusion
  785.7 0.2 dynamic-update-slice.3
  786.0 13.2 %all-reduce.4 = (f32[256]{0:T(256)S(1)}, f32[256]{0:T(256)S(1)}) all-reduce(f32[256]{0:T(256)S(1)} %dynamic-update-slice.2, f32[256]{0:T(256)S(1)} %dynamic-update-slice.3), channel_id=4, replica_groups=mesh['fac'=8,'loc'=4] {'fac'}, use_global_device_ids=true, to_apply=%add.2 | all-reduce | flops 512 | bytes 4096
  799.2 0.1 reshape.51
  799.2 0.1 reshape.50
  799.3 0.3 while.35
  799.6 0.7 subtract_subtract_fusion
  800.3 0.0 all-to-all-done.3
  800.3 48.8 %join.1 = f32[16,32,128,128]{3,2,1,0:T(8,128)} custom-call(f32[8,4,1,4,32,128]{5,4,3,2,1,0:T(8,128)S(1)} %bitcast.46, f32[8,4,2,4,32,128]{5,4,3,2,1,0:T(8,128)} %bitcast.9.refs_1_, f32[8,4,4,4,32,128]{5,4,3,2,1,0:T(8,128)} %bitcast.11.refs_2_, f32[8,4,9,4,32,128]{5,4,3,2,1,0:T(8,128)} %bitcast.13.refs_3_, f32[16,32,128,128]{3,2,1,0:T(8,128)} %bitcast.50), custom_call_target="tpu_custom_call" | custom-call | flops 33554432 | bytes 100663296 | tf_op jit(solution)/shard_map/join/pallas_call | solution.py:222
  (20 shorter events, 0.3 us)
Async XLA Ops:
  18.4 1.3 copy-start.3
  19.7 51.7 %all-to-all-start = ((f32[32,1,4,32,128]{4,3,2,1,0:T(8,128)}), f32[32,1,4,32,128]{4,3,2,1,0:T(8,128)S(1)}, u32[]{:S(2)}, u32[]{:S(2)}) async-start(f32[32,1,4,32,128]{4,3,2,1,0:T(8,128)} %bitcast.49), calls=%async_computation | async-start | bytes 4194304 | tf_op jit(solution)/shard_map/all_to_all | solution.py:266
  59.8 2.0 copy-start.2
  71.4 95.5 %all-to-all-start.1 = ((f32[32,2,4,32,128]{4,3,2,1,0:T(8,128)}), f32[32,2,4,32,128]{4,3,2,1,0:T(8,128)}, u32[]{:S(2)}, u32[]{:S(2)}) async-start(f32[32,2,4,32,128]{4,3,2,1,0:T(8,128)} %bitcast.48), calls=%async_computation.1 | async-start | bytes 8388608 | tf_op jit(solution)/shard_map/all_to_all | solution.py:266
  143.6 3.2 copy-start.1
  166.9 185.4 %all-to-all-start.2 = ((f32[32,4,4,32,128]{4,3,2,1,0:T(8,128)}), f32[32,4,4,32,128]{4,3,2,1,0:T(8,128)}, u32[]{:S(2)}, u32[]{:S(2)}) async-start(f32[32,4,4,32,128]{4,3,2,1,0:T(8,128)} %bitcast.47), calls=%async_computation.2 | async-start | bytes 16777216 | tf_op jit(solution)/shard_map/all_to_all | solution.py:266
  321.9 6.8 copy-start
  352.3 13.3 %copy-start.6 = (u32[32]{0:T(128)S(1)}, u32[32]{0:T(128)}, u32[]{:S(2)}) copy-start(u32[32]{0:T(128)} %constant.96) | copy-start | bytes 388
  352.3 14.0 %copy-start.5 = (u32[32]{0:T(128)S(1)}, u32[32]{0:T(128)}, u32[]{:S(2)}) copy-start(u32[32]{0:T(128)} %constant.86) | copy-start | bytes 388
  352.3 15.6 %copy-start.4 = (f32[16,32]{1,0:T(8,128)S(1)}, f32[16,32]{1,0:T(8,128)}, u32[]{:S(2)}) copy-start(f32[16,32]{1,0:T(8,128)} %param.7) | copy-start | bytes 6148
  352.3 448.0 %all-to-all-start.3 = ((f32[32,9,4,32,128]{4,3,2,1,0:T(8,128)}), f32[32,9,4,32,128]{4,3,2,1,0:T(8,128)}, u32[]{:S(2)}, u32[]{:S(2)}) async-start(f32[32,9,4,32,128]{4,3,2,1,0:T(8,128)} %bitcast.45), calls=%async_computation.3 | async-start | bytes 37748736 | tf_op jit(solution)/shard_map/all_to_all | solution.py:266
